TPU v7x, 32 devices: a whole 2x2x4 slice. The times are simulated.
32 devices in a mesh: grp: 4 (over y, x), vid: 8 (over z, core).
Axes of the slice: x: 2, y: 2, z: 4, core: 2. Of those that a mesh axis runs over, the one named last changes fastest.
Arguments:
- frames: bfloat16 [32768, 1024], P(('grp', 'vid')), parts along dimension 0, may hold values from -240 to 240
- w_frame: bfloat16 [1024, 512], replicated, may hold values from -0.1875 to 0.1875
- step_emb: bfloat16 [4096, 512], P(('grp', 'vid')), parts along dimension 0, may hold values from -6 to 6
- targets: int32 [32768], P(('grp', 'vid')), parts along dimension 0, may hold values from 0 to 127
- tile_frame: int32 [32, 64], P(('grp', 'vid')), parts along dimension 0, may hold values from 0 to 7, as said below
- tile_step: int32 [32, 64], P(('grp', 'vid')), parts along dimension 0, may hold values from 0 to 7, as said below
- tile_count: int32 [32], P(('grp', 'vid')), parts along dimension 0, may hold values from 8 to 64, as said below
Outputs:
- row_loss: float32 [32768], P(('grp', 'vid')), parts along dimension 0
- frame_grad: bfloat16 [32768, 1024], P(('grp', 'vid')), parts along dimension 0
- step_grad: float32 [4096, 512], P(('grp', 'vid')), parts along dimension 0
There are 4 independent parts, one for each index of `grp`. A program takes and returns all parts, laid end to end along the dimension named above; an argument that names none is the same for every part. Nothing has to cross between parts.
Inputs may be any that keep to these rules, and one draw needn't show every extreme that they name: `tile_frame`: each run of 8 tiles of a list, starting at a multiple of 8, names every frame block once. `tile_step`: the (frame block, step block) pairs of one video's list are distinct; the first 8 tiles pair each frame block with the video's own step block. Only the first tile_count tiles of a list are valid; some video's list is full.
All inputs are finite; a program needn't handle non-finite values.
Results may differ from a plain program's by a relative error of at most 0.0086.
Values may be sent and summed in bfloat16 or wider, within the bound.
No kernel may reach another device: no remote copies, remote signals or barrier semaphores. Data moves between devices by JAX's collectives and lax.ppermute only.
A program may use at most 128 MiB of HBM per device.

v0:
```python
import math

import jax
import jax.numpy as jnp
from jax import lax
from jax.experimental import pallas as pl
from jax.experimental.pallas import tpu as pltpu
from jax.sharding import PartitionSpec as P

F32 = jnp.float32
BF16 = jnp.bfloat16
HIDDEN = -1e30
EMBED_MIB = 52
TILES = 4
NT = (((1,), (1,)), ((), ()))
TN = (((0,), (0,)), ((), ()))
VMEM = pl.BlockSpec(memory_space=pltpu.VMEM)
SMEM = pl.BlockSpec(memory_space=pltpu.SMEM)


def params(mib):
    return pltpu.CompilerParams(vmem_limit_bytes=mib * 2**20)


def cost(flops, nbytes, exps=0, scale=1):
    return pl.CostEstimate(
        flops=flops // scale, bytes_accessed=nbytes // scale, transcendentals=exps // scale
    )


def embed_kernel(x_hbm, w_hbm, e_ref, x_ref, w_ref, sem):
    tile = x_ref.shape[0] // TILES
    deep = w_ref.shape[0] // TILES
    reads = []
    for n in range(TILES):
        at = pl.ds(n * deep, deep)
        reads.append(pltpu.make_async_copy(w_hbm.at[at], w_ref.at[at], sem.at[n]))
    for n in range(TILES):
        at = pl.ds(n * tile, tile)
        reads.append(pltpu.make_async_copy(x_hbm.at[at], x_ref.at[at], sem.at[TILES + n]))
    for read in reads:
        read.start()
    for read in reads[:TILES]:
        read.wait()
    for n in range(TILES):
        reads[TILES + n].wait()
        at = slice(n * tile, (n + 1) * tile)
        e_ref[at, :] = jnp.dot(x_ref[at, :], w_ref[...], preferred_element_type=F32).astype(BF16)


def embed(frames, w):
    rows, depth = frames.shape
    width = w.shape[1]
    return pl.pallas_call(
        embed_kernel,
        in_specs=[pl.BlockSpec(memory_space=pl.ANY)] * 2,
        out_specs=VMEM,
        out_shape=jax.ShapeDtypeStruct((rows, width), BF16),
        scratch_shapes=[
            pltpu.VMEM((rows, depth), BF16),
            pltpu.VMEM((depth, width), BF16),
            pltpu.SemaphoreType.DMA((2 * TILES,)),
        ],
        cost_estimate=cost(2 * rows * depth * width, 2 * (rows * depth + depth * width + rows * width)),
        compiler_params=params(EMBED_MIB),
        name="embed",
    )(frames, w)


def sight(place, count, tf, ts, shape):
    videos, rows = shape
    slots = tf.shape[1]
    line = lax.broadcasted_iota(jnp.int32, (videos, slots), 0)
    slot = lax.broadcasted_iota(jnp.int32, (videos, slots), 1)
    video = line ^ place
    left = jnp.where((ts == video) & (slot < count), 1.0, 0.0)
    block = lax.broadcasted_iota(jnp.int32, (rows, slots), 0) // 128
    right = jnp.where(tf == block, 1.0, 0.0)
    seen = lax.dot_general(left.astype(BF16), right.astype(BF16), NT, preferred_element_type=F32)
    return jnp.where(seen > 0.5, 0.0, HIDDEN)


def stack(refs):
    values = [ref[...] for ref in refs]
    return values[0] if len(values) == 1 else jnp.concatenate(values, axis=0)


def tiles(rows):
    return [slice(at, at + 256) for at in range(0, rows, 256)]


def score_kernel(k, parts, temper, *refs):
    e_ref = refs[0]
    blocks = refs[1 : 1 + parts]
    if k == 0:
        place_ref, count_ref, tf_ref, ts_ref, goal_ref = refs[1 + parts : 6 + parts]
        p_ref, top_ref, total_ref, pos_ref, bias_ref = refs[6 + parts :]
        bias_ref[...] = sight(place_ref[0], count_ref[0], tf_ref[...], ts_ref[...], bias_ref.shape)
    else:
        bias_ref, top_in, total_in, p_ref, top_ref, total_ref = refs[1 + parts :]
    chunk = stack(blocks)
    steps = chunk.shape[0]
    own = steps // 2
    for at in tiles(e_ref.shape[0]):
        s = lax.dot_general(chunk, e_ref[at, :], NT, preferred_element_type=F32) * temper
        bias = bias_ref[2 * k : 2 * k + 2, at]
        first, second = s[:own] + bias[0:1], s[own:] + bias[1:2]
        top = jnp.maximum(
            jnp.max(first, axis=0, keepdims=True), jnp.max(second, axis=0, keepdims=True)
        )
        if k == 0:
            hit = goal_ref[:, at] == lax.broadcasted_iota(jnp.int32, first.shape, 0)
            pos_ref[:, at] = jnp.sum(jnp.where(hit, s[:own], 0.0), axis=0, keepdims=True)
        else:
            top = jnp.maximum(top, top_in[:, at])
        first, second = jnp.exp(first - top), jnp.exp(second - top)
        p_ref[:own, at] = first
        p_ref[own:, at] = second
        total = jnp.sum(first, axis=0, keepdims=True) + jnp.sum(second, axis=0, keepdims=True)
        if k > 0:
            total = total + total_in[:, at] * jnp.exp(top_in[:, at] - top)
        top_ref[:, at] = top
        total_ref[:, at] = total


def score(k, videos, temper, e, chunk, *more):
    rows, width = e.shape
    steps = sum(part.shape[0] for part in chunk)
    line = jax.ShapeDtypeStruct((1, rows), F32)
    extra = [line, jax.ShapeDtypeStruct((videos, rows), F32)] if k == 0 else []
    specs = [SMEM, SMEM, VMEM, VMEM, VMEM] if k == 0 else [VMEM] * len(more)
    return pl.pallas_call(
        lambda *refs: score_kernel(k, len(chunk), temper, *refs),
        in_specs=[VMEM] * (1 + len(chunk)) + specs,
        out_specs=[VMEM] * (3 + len(extra)),
        out_shape=[jax.ShapeDtypeStruct((steps, rows), F32), line, line] + extra,
        cost_estimate=cost(
            2 * steps * rows * width, 2 * (rows + steps) * width + 4 * steps * rows, steps * rows
        ),
        compiler_params=params(24),
        name=f"score_{k}",
    )(e, *chunk, *more)


def share_kernel(ks, *refs):
    last_ref, total_ref, e_ref = refs[:3]
    ins, outs = refs[3 : 3 + 2 * len(ks)], refs[3 + 2 * len(ks) :]
    if 0 in ks:
        goal_ref, pos_ref = outs[:2]
        outs[-1][...] = last_ref[...] + jnp.log(total_ref[...]) - pos_ref[...]
        outs = outs[2:]
    for n, k in enumerate(ks):
        p_ref, top_ref = ins[2 * n : 2 * n + 2]
        q_ref, mine_ref, other_ref = outs[3 * n : 3 * n + 3]
        own = mine_ref.shape[0]
        scale = jnp.exp(top_ref[...] - last_ref[...]) / total_ref[...]
        out = None
        for at in tiles(e_ref.shape[0]):
            q = (p_ref[:, at] * scale[:, at]).astype(BF16)
            if k == 0:
                hit = goal_ref[:, at] == lax.broadcasted_iota(jnp.int32, (own, q.shape[1]), 0)
                first = (q[:own].astype(F32) - jnp.where(hit, 1.0, 0.0)).astype(BF16)
                q = jnp.concatenate([first, q[own:]], axis=0)
            q_ref[:, at] = q
            part = jnp.dot(q, e_ref[at, :], preferred_element_type=F32)
            out = part if out is None else out + part
        mine_ref[...] = out[:own]
        other_ref[...] = out[own:].astype(BF16)


def share(ks, kept, last, total, e, *more):
    steps, rows = kept[ks[0]][0].shape
    width = e.shape[1]
    own = steps // 2
    each = [
        jax.ShapeDtypeStruct((steps, rows), BF16),
        jax.ShapeDtypeStruct((own, width), F32),
        jax.ShapeDtypeStruct((own, width), BF16),
    ]
    shapes = each * len(ks) + [jax.ShapeDtypeStruct((1, rows), F32)] * (0 in ks)
    ins = [part for k in ks for part in kept[k]]
    return pl.pallas_call(
        lambda *refs: share_kernel(ks, *refs),
        in_specs=[VMEM] * (3 + len(ins) + len(more)),
        out_specs=[VMEM] * len(shapes),
        out_shape=shapes,
        cost_estimate=cost(
            2 * len(ks) * steps * rows * width, len(ks) * 6 * steps * rows + 2 * rows * width
        ),
        compiler_params=params(24),
        name=f"share_{ks[0]}",
    )(last, total, e, *ins, *more)


def rows_kernel(sizes, temper, *refs):
    n = len(sizes)
    out_ref = refs[-1]
    at = n
    chunks = []
    for size in sizes:
        chunks.append(stack(refs[at : at + size]))
        at += size
    for cut in tiles(out_ref.shape[0]):
        rows = None
        for q_ref, chunk in zip(refs[:n], chunks):
            part = lax.dot_general(q_ref[:, cut], chunk, TN, preferred_element_type=F32)
            rows = part if rows is None else rows + part
        out_ref[cut, :] = (rows * temper).astype(BF16)


def rows_of(qs, chunks, temper):
    n = len(qs)
    steps, rows = qs[0].shape
    flat = [part for chunk in chunks for part in chunk]
    width = flat[0].shape[1]
    return pl.pallas_call(
        lambda *refs: rows_kernel([len(chunk) for chunk in chunks], temper, *refs),
        in_specs=[VMEM] * (n + len(flat)),
        out_specs=VMEM,
        out_shape=jax.ShapeDtypeStruct((rows, width), BF16),
        cost_estimate=cost(2 * rows * width * n * steps, 2 * n * steps * (rows + width)),
        compiler_params=params(24),
        name="rows",
    )(*qs, *flat)


def back_kernel(g_ref, w_ref, out_hbm, out_ref, sem):
    tile = out_ref.shape[0] // TILES
    writes = []
    for n in range(TILES):
        at = slice(n * tile, (n + 1) * tile)
        out_ref[at, :] = lax.dot_general(
            g_ref[at, :], w_ref[...], NT, preferred_element_type=F32
        ).astype(BF16)
        at = pl.ds(n * tile, tile)
        writes.append(pltpu.make_async_copy(out_ref.at[at], out_hbm.at[at], sem.at[n]))
        writes[n].start()
    for write in writes:
        write.wait()


def back(g, w):
    rows, width = g.shape
    depth = w.shape[0]
    return pl.pallas_call(
        back_kernel,
        in_specs=[VMEM, VMEM],
        out_specs=pl.BlockSpec(memory_space=pl.ANY),
        out_shape=jax.ShapeDtypeStruct((rows, depth), BF16),
        scratch_shapes=[pltpu.VMEM((rows, depth), BF16), pltpu.SemaphoreType.DMA((TILES,))],
        cost_estimate=cost(2 * rows * width * depth, 2 * (depth * width + rows * (width + depth))),
        compiler_params=params(40),
        name="back",
    )(g, w)


def shards(frames, w_frame, step_emb, targets, tile_frame, tile_step, tile_count):
    videos = lax.axis_size("vid")
    chips = videos // 2
    temper = 1.0 / math.sqrt(step_emb.shape[1])
    place = lax.axis_index("vid").astype(jnp.int32)

    def trade(x, k):
        return lax.ppermute(x, "vid", [(i, i ^ k) for i in range(videos)])

    goals = targets.reshape(1, -1)
    e = embed(frames, w_frame)
    found = trade(step_emb, 1)
    mine = {0: step_emb}
    order, bit = [0], chips // 2
    while bit:
        order += [k ^ bit for k in order]
        bit //= 2
    chunks, kept = {}, {}
    more = (place.reshape(1), tile_count, tile_frame, tile_step, goals)
    for n, k in enumerate(order):
        chunks[k] = [mine[k], found if k == 0 else trade(mine[k], 1)]
        if n + 1 < chips:
            coming = order[n + 1]
            low = coming & -coming
            come = trade(mine[coming ^ low], 2 * low)
            mine[coming], gate = lax.optimization_barrier((come, e if n == 0 else top))
        p, top, total, *first = score(k, videos, temper, e, chunks[k], *more)
        kept[k] = (p, top)
        if k == 0:
            pos, bias = first
        more = (bias, top, total)
    last = top

    qs, sums = {}, {}
    sequence = [(k,) for k in range(chips - 1, 1, -1)] + [(1, 0)]
    for n, ks in enumerate(sequence):
        for m in range(n - 1, max(n - 3, -1), -1):
            k = sequence[m][0]
            if m == n - 1:
                e, qs[k] = lax.optimization_barrier((e, qs[k]))
            else:
                e, sums[k] = lax.optimization_barrier((e, sums[k]))
        made = share(ks, kept, last, total, e, *((goals, pos) if 0 in ks else ()))
        for m, k in enumerate(ks):
            qs[k], part, other = made[3 * m : 3 * m + 3]
            sums[k] = part + trade(other, 1).astype(F32)
    loss = made[-1]
    g = rows_of([qs[k] for k in order], [chunks[k] for k in order], temper)
    sums[1], g = lax.optimization_barrier((sums[1], g))
    bit = 1
    while bit < chips:
        for k in range(chips - bit, 0, -2 * bit):
            sums[k - bit] = sums[k - bit] + trade(sums[k].astype(BF16), 2 * bit).astype(F32)
        bit *= 2
    frame_grad = back(g, w_frame)
    return (loss.reshape(-1), frame_grad, sums[0] * temper)


def solution(mesh):
    placed = (
        P(("grp", "vid"), None),
        P(),
        P(("grp", "vid"), None),
        P(("grp", "vid")),
        P(("grp", "vid"), None),
        P(("grp", "vid"), None),
        P(("grp", "vid")),
    )
    return jax.shard_map(
        shards,
        mesh=mesh,
        in_specs=placed,
        out_specs=(P(("grp", "vid")), P(("grp", "vid"), None), P(("grp", "vid"), None)),
        check_vma=False,
    )
```

profile of v0, /device:TPU:0, one launch (start us, length us, event | category | flops | bytes accessed | tf_op | source)
XLA Modules:
  0.0 36.5 jit_solution(4851057977409914747)
XLA Ops:
  0.7 4.1 %collective-permute-start = (bf16[128,512]{1,0:T(8,128)(2,1)}, bf16[128,512]{1,0:T(8,128)(2,1)S(1)}, u32[]{:S(2)}, u32[]{:S(2)}) collective-permute-start(bf16[128,512]{1,0:T(8,128)(2,1)} %refs_4_.2), channel_id=1, source_target_pairs={{0,4},{1,5},{2,6},{3,7},{4,0},{5,1},{6,2},{7,3},{8,12},{9,13},{10,... | collective-permute-start | bytes 393224 | tf_op jit(solution)/shard_map/ppermute | solution.py:264
  4.8 0.0 collective-permute-start.3
  4.8 1.6 %collective-permute-start.5 = (bf16[128,512]{1,0:T(8,128)(2,1)}, bf16[128,512]{1,0:T(8,128)(2,1)S(1)}, u32[]{:S(2)}, u32[]{:S(2)}) collective-permute-start(bf16[128,512]{1,0:T(8,128)(2,1)} %refs_4_.2), channel_id=1, source_target_pairs={{0,2},{1,3},{2,0},{3,1},{4,6},{5,7},{6,4},{7,5},{8,10},{9,11},{10,... | collective-permute-start | bytes 393224 | tf_op jit(solution)/shard_map/ppermute | solution.py:264
  6.4 3.2 %embed.1.refs_0_.refs_2_ = bf16[1024,512]{1,0:T(8,128)(2,1)S(1)} custom-call(bf16[1024,1024]{1,0:T(8,128)(2,1)} %x_hbm.1, bf16[1024,512]{1,0:T(8,128)(2,1)} %w_ref.1), custom_call_target="tpu_custom_call" | custom-call | flops 1073741824 | bytes 4194304 | tf_op jit(solution)/shard_map/embed/pallas_call | solution.py:54
  9.5 1.9 %collective-permute-done.refs_1_.refs_6_ = bf16[128,512]{1,0:T(8,128)(2,1)S(1)} collective-permute-done((bf16[128,512]{1,0:T(8,128)(2,1)}, bf16[128,512]{1,0:T(8,128)(2,1)S(1)}, u32[]{:S(2)}, u32[]{:S(2)}) %collective-permute-start) | collective-permute-done | bytes 131104 | tf_op jit(solution)/shard_map/ppermute | solution.py:264
  11.4 0.0 collective-permute-start.2
  11.4 0.8 %collective-permute-start.1 = (bf16[128,512]{1,0:T(8,128)(2,1)S(1)}, bf16[128,512]{1,0:T(8,128)(2,1)S(1)}, u32[]{:S(2)}, u32[]{:S(2)}) collective-permute-start(bf16[128,512]{1,0:T(8,128)(2,1)S(1)} %collective-permute-done.refs_1_.refs_6_), channel_id=1, source_target_pairs={{0,2},{1,3},{2,0},{3,1},{4,6},{5,7},{6,4},{7,5},{8,10},{9,11},{10,... | collective-permute-start | bytes 393224 | tf_op jit(solution)/shard_map/ppermute | solution.py:264
  12.9 0.7 %score_0.1 = (f32[256,1024]{1,0:T(8,128)S(1)}, f32[1,1024]{1,0:T(1,128)S(1)}, f32[1,1024]{1,0:T(1,128)S(1)}, f32[1,1024]{1,0:T(1,128)S(1)}, f32[8,1024]{1,0:T(8,128)S(1)}) custom-call(bf16[1024,512]{1,0:T(8,128)(2,1)S(1)} %embed.1.refs_0_.refs_2_, bf16[128,512]{1,0:T(8,128)(2,1)S(1)} %copy-done.1, ...), custom_call_target="tpu_custom_call" | custom-call | flops 268435456 | bytes 2359296 | tf_op jit(solution)/shard_map/score_0/pallas_call | solution.py:132
  13.6 0.0 collective-permute-done.5.refs_1_.refs_8_
  13.6 0.3 collective-permute-start.6
  13.9 0.0 collective-permute-done.2.refs_2_.refs_7_
  13.9 0.6 %score_2.1 = (f32[256,1024]{1,0:T(8,128)S(1)}, f32[1,1024]{1,0:T(1,128)S(1)}, f32[1,1024]{1,0:T(1,128)S(1)}) custom-call(bf16[1024,512]{1,0:T(8,128)(2,1)S(1)} %embed.1.refs_0_.refs_2_, bf16[128,512]{1,0:T(8,128)(2,1)S(1)} %collective-permute-done.refs_1_.refs_6_, bf16[128,512]{1,0:T(8,128)(2,1)S(1)} %collective-permute-done.2.refs_2_.refs_7_, ...), custom_call_target="tpu_custom_call" | custom-call | flops 268435456 | bytes 2359296 | tf_op jit(solution)/shard_map/score_2/pallas_call | solution.py:132
  14.5 2.8 %collective-permute-done.1.refs_1_.refs_10_ = bf16[128,512]{1,0:T(8,128)(2,1)S(1)} collective-permute-done((bf16[128,512]{1,0:T(8,128)(2,1)S(1)}, bf16[128,512]{1,0:T(8,128)(2,1)S(1)}, u32[]{:S(2)}, u32[]{:S(2)}) %collective-permute-start.1) | collective-permute-done | bytes 131104 | tf_op jit(solution)/shard_map/ppermute | solution.py:264
  17.3 0.6 %score_1.1 = (f32[256,1024]{1,0:T(8,128)S(1)}, f32[1,1024]{1,0:T(1,128)S(1)}, f32[1,1024]{1,0:T(1,128)S(1)}) custom-call(bf16[1024,512]{1,0:T(8,128)(2,1)S(1)} %embed.1.refs_0_.refs_2_, bf16[128,512]{1,0:T(8,128)(2,1)S(1)} %collective-permute-done.5.refs_1_.refs_8_, bf16[128,512]{1,0:T(8,128)(2,1)S(1)} %collective-permute-done.6.refs_2_.refs_9_, ...), custom_call_target="tpu_custom_call" | custom-call | flops 268435456 | bytes 2359296 | tf_op jit(solution)/shard_map/score_1/pallas_call | solution.py:132
  17.9 0.8 %collective-permute-done.4.refs_2_.refs_11_ = bf16[128,512]{1,0:T(8,128)(2,1)S(1)} collective-permute-done((bf16[128,512]{1,0:T(8,128)(2,1)S(1)}, bf16[128,512]{1,0:T(8,128)(2,1)S(1)}, u32[]{:S(2)}, u32[]{:S(2)}) %collective-permute-start.4) | collective-permute-done | bytes 131104 | tf_op jit(solution)/shard_map/ppermute | solution.py:264
  18.7 0.6 %score_3.1 = (f32[256,1024]{1,0:T(8,128)S(1)}, f32[1,1024]{1,0:T(1,128)S(1)}, f32[1,1024]{1,0:T(1,128)S(1)}) custom-call(bf16[1024,512]{1,0:T(8,128)(2,1)S(1)} %embed.1.refs_0_.refs_2_, bf16[128,512]{1,0:T(8,128)(2,1)S(1)} %collective-permute-done.1.refs_1_.refs_10_, bf16[128,512]{1,0:T(8,128)(2,1)S(1)} %collective-permute-done.4.refs_2_.refs_11_, ...), custom_call_target="tpu_custom_call" | custom-call | flops 268435456 | bytes 2359296 | tf_op jit(solution)/shard_map/score_3/pallas_call | solution.py:132
  19.2 0.4 %share_3.1 = (bf16[256,1024]{1,0:T(8,128)(2,1)S(1)}, f32[128,512]{1,0:T(8,128)S(1)}, bf16[128,512]{1,0:T(8,128)(2,1)S(1)}) custom-call(f32[1,1024]{1,0:T(1,128)S(1)} %get-tuple-element.51.refs_0_.refs_4_, f32[1,1024]{1,0:T(1,128)S(1)} %get-tuple-element.52.refs_1_, bf16[1024,512]{1,0:T(8,128)(2,1)S(1)} %embed.1.refs_0_.refs_2_, ...), custom_call_target="tpu_custom_call" | custom-call | flops 268435456 | bytes 2621440 | tf_op jit(solution)/shard_map/share_3/pallas_call | solution.py:182
  19.7 0.2 collective-permute-start.7
  19.9 0.5 %share_2.1 = (bf16[256,1024]{1,0:T(8,128)(2,1)S(1)}, f32[128,512]{1,0:T(8,128)S(1)}, bf16[128,512]{1,0:T(8,128)(2,1)S(1)}) custom-call(f32[1,1024]{1,0:T(1,128)S(1)} %get-tuple-element.51.refs_0_.refs_4_, f32[1,1024]{1,0:T(1,128)S(1)} %get-tuple-element.52.refs_1_, bf16[1024,512]{1,0:T(8,128)(2,1)S(1)} %embed.1.refs_0_.refs_2_, ...), custom_call_target="tpu_custom_call" | custom-call | flops 268435456 | bytes 2621440 | tf_op jit(solution)/shard_map/share_2/pallas_call | solution.py:182
  20.4 0.4 %collective-permute-start.11 = (bf16[128,512]{1,0:T(8,128)(2,1)S(1)}, bf16[128,512]{1,0:T(8,128)(2,1)S(1)}, u32[]{:S(2)}, u32[]{:S(2)}) collective-permute-start(bf16[128,512]{1,0:T(8,128)(2,1)S(1)} %get-tuple-element.77), channel_id=1, source_target_pairs={{0,1},{1,0},{2,3},{3,2},{4,5},{5,4},{6,7},{7,6},{8,9},{9,8},{10,11... | collective-permute-start | bytes 393224 | tf_op jit(solution)/shard_map/ppermute | solution.py:264
  20.8 0.3 collective-permute-done.7
  21.1 0.8 %collective-permute-start.12 = (bf16[128,512]{1,0:T(8,128)(2,1)S(1)}, bf16[128,512]{1,0:T(8,128)(2,1)S(1)}, u32[]{:S(2)}, u32[]{:S(2)}) collective-permute-start(bf16[128,512]{1,0:T(8,128)(2,1)S(1)} %convert_add_fusion.1), channel_id=1, source_target_pairs={{0,2},{1,3},{2,0},{3,1},{4,6},{5,7},{6,4},{7,5},{8,10},{9,11},{10,... | collective-permute-start | bytes 393224 | tf_op jit(solution)/shard_map/ppermute | solution.py:264
  22.0 1.1 %share_1.1 = (bf16[256,1024]{1,0:T(8,128)(2,1)S(1)}, f32[128,512]{1,0:T(8,128)S(1)}, bf16[128,512]{1,0:T(8,128)(2,1)S(1)}, bf16[256,1024]{1,0:T(8,128)(2,1)S(1)}...) custom-call(f32[1,1024]{1,0:T(1,128)S(1)} %get-tuple-element.51.refs_0_.refs_4_, ...), custom_call_target="tpu_custom_call" | custom-call | flops 536870912 | bytes 4194304 | tf_op jit(solution)/shard_map/share_1/pallas_call | solution.py:182
  23.1 0.5 %collective-permute-start.9 = (bf16[128,512]{1,0:T(8,128)(2,1)S(1)}, bf16[128,512]{1,0:T(8,128)(2,1)S(1)}, u32[]{:S(2)}, u32[]{:S(2)}) collective-permute-start(bf16[128,512]{1,0:T(8,128)(2,1)S(1)} %get-tuple-element.74), channel_id=1, source_target_pairs={{0,1},{1,0},{2,3},{3,2},{4,5},{5,4},{6,7},{7,6},{8,9},{9,8},{10,11... | collective-permute-start | bytes 393224 | tf_op jit(solution)/shard_map/ppermute | solution.py:264
  23.6 1.3 %rows.1.g_ref = bf16[1024,512]{1,0:T(8,128)(2,1)S(1)} custom-call(bf16[256,1024]{1,0:T(8,128)(2,1)S(1)} %get-tuple-element.68.refs_0_, bf16[256,1024]{1,0:T(8,128)(2,1)S(1)} %get-tuple-element.69.refs_1_, bf16[256,1024]{1,0:T(8,128)(2,1)S(1)} %get-tuple-element.70.refs_2_, bf16[256,1024]{1,0:T(8,128)(2,1)S(1)} %get-tuple-element.71.refs_3_, ...), custom_call_target="tpu_custom_call" | custom-call | flops 1073741824 | bytes 3145728 | tf_op jit(solution)/shard_map/rows/pallas_call | solution.py:216
  24.9 1.8 %collective-permute-done.12 = bf16[128,512]{1,0:T(8,128)(2,1)S(1)} collective-permute-done((bf16[128,512]{1,0:T(8,128)(2,1)S(1)}, bf16[128,512]{1,0:T(8,128)(2,1)S(1)}, u32[]{:S(2)}, u32[]{:S(2)}) %collective-permute-start.12) | collective-permute-done | bytes 131104 | tf_op jit(solution)/shard_map/ppermute | solution.py:264
  26.8 2.4 %collective-permute-start.13 = (bf16[128,512]{1,0:T(8,128)(2,1)S(1)}, bf16[128,512]{1,0:T(8,128)(2,1)S(1)}, u32[]{:S(2)}, u32[]{:S(2)}) collective-permute-start(bf16[128,512]{1,0:T(8,128)(2,1)S(1)} %add_convert_fusion), channel_id=1, source_target_pairs={{0,4},{1,5},{2,6},{3,7},{4,0},{5,1},{6,2},{7,3},{8,12},{9,13},{10,... | collective-permute-start | bytes 393224 | tf_op jit(solution)/shard_map/ppermute | solution.py:264
  29.3 1.8 %collective-permute-start.10 = (bf16[128,512]{1,0:T(8,128)(2,1)S(1)}, bf16[128,512]{1,0:T(8,128)(2,1)S(1)}, u32[]{:S(2)}, u32[]{:S(2)}) collective-permute-start(bf16[128,512]{1,0:T(8,128)(2,1)S(1)} %convert_add_fusion), channel_id=1, source_target_pairs={{0,2},{1,3},{2,0},{3,1},{4,6},{5,7},{6,4},{7,5},{8,10},{9,11},{10,... | collective-permute-start | bytes 393224 | tf_op jit(solution)/shard_map/ppermute | solution.py:264
  31.1 2.1 %back.1 = bf16[1024,1024]{1,0:T(8,128)(2,1)} custom-call(bf16[1024,512]{1,0:T(8,128)(2,1)S(1)} %rows.1.g_ref, bf16[1024,512]{1,0:T(8,128)(2,1)S(1)} %copy-done), custom_call_target="tpu_custom_call" | custom-call | flops 1073741824 | bytes 4194304 | tf_op jit(solution)/shard_map/back/pallas_call | solution.py:245
  33.2 2.2 %collective-permute-done.13 = bf16[128,512]{1,0:T(8,128)(2,1)S(1)} collective-permute-done((bf16[128,512]{1,0:T(8,128)(2,1)S(1)}, bf16[128,512]{1,0:T(8,128)(2,1)S(1)}, u32[]{:S(2)}, u32[]{:S(2)}) %collective-permute-start.13) | collective-permute-done | bytes 131104 | tf_op jit(solution)/shard_map/ppermute | solution.py:264
  35.4 0.3 collective-permute-done.10
  35.8 0.8 %add_multiply_fusion = f32[128,512]{1,0:T(8,128)} fusion(bf16[128,512]{1,0:T(8,128)(2,1)S(1)} %collective-permute-done.13, bf16[128,512]{1,0:T(8,128)(2,1)S(1)} %collective-permute-done.10, f32[128,512]{1,0:T(8,128)S(1)} %get-tuple-element.73, bf16[128,512]{1,0:T(8,128)(2,1)S(1)} %collective-permute-done.9), kind=kLoop, calls=%fused_computation | loop fusion | flops 458752 | bytes 917504 | tf_op jit(solution)/shard_map/mul | solution.py:312
  (20 shorter events, 0.1 us)
Async XLA Ops:
  0.6 12.2 %copy-start.1 = (bf16[128,512]{1,0:T(8,128)(2,1)S(1)}, bf16[128,512]{1,0:T(8,128)(2,1)}, u32[]{:S(2)}) copy-start(bf16[128,512]{1,0:T(8,128)(2,1)} %refs_4_.2) | copy-start | bytes 393220
  0.6 12.2 %copy-start.2 = (s32[1024]{0:T(1024)S(1)}, s32[1024]{0:T(1024)}, u32[]{:S(2)}) copy-start(s32[1024]{0:T(1024)} %param.10) | copy-start | bytes 12292
  0.7 12.2 %copy-start.3 = (s32[1,64]{1,0:T(1,128)S(1)}, s32[1,64]{1,0:T(1,128)}, u32[]{:S(2)}) copy-start(s32[1,64]{1,0:T(1,128)} %refs_5_.1) | copy-start | bytes 772
  0.7 12.2 %copy-start.4 = (s32[1,64]{1,0:T(1,128)S(1)}, s32[1,64]{1,0:T(1,128)}, u32[]{:S(2)}) copy-start(s32[1,64]{1,0:T(1,128)} %refs_6_.1) | copy-start | bytes 772
  0.7 10.7 %collective-permute-start = (bf16[128,512]{1,0:T(8,128)(2,1)}, bf16[128,512]{1,0:T(8,128)(2,1)S(1)}, u32[]{:S(2)}, u32[]{:S(2)}) collective-permute-start(bf16[128,512]{1,0:T(8,128)(2,1)} %refs_4_.2), channel_id=1, source_target_pairs={{0,4},{1,5},{2,6},{3,7},{4,0},{5,1},{6,2},{7,3},{8,12},{9,13},{10,... | collective-permute-start | bytes 393224 | tf_op jit(solution)/shard_map/ppermute | solution.py:264
  4.8 8.1 %collective-permute-start.3 = (bf16[128,512]{1,0:T(8,128)(2,1)}, bf16[128,512]{1,0:T(8,128)(2,1)S(1)}, u32[]{:S(2)}, u32[]{:S(2)}) collective-permute-start(bf16[128,512]{1,0:T(8,128)(2,1)} %refs_4_.2), channel_id=1, source_target_pairs={{0,1},{1,0},{2,3},{3,2},{4,5},{5,4},{6,7},{7,6},{8,9},{9,8},{10,11... | collective-permute-start | bytes 393224 | tf_op jit(solution)/shard_map/ppermute | solution.py:264
  4.8 8.8 %collective-permute-start.5 = (bf16[128,512]{1,0:T(8,128)(2,1)}, bf16[128,512]{1,0:T(8,128)(2,1)S(1)}, u32[]{:S(2)}, u32[]{:S(2)}) collective-permute-start(bf16[128,512]{1,0:T(8,128)(2,1)} %refs_4_.2), channel_id=1, source_target_pairs={{0,2},{1,3},{2,0},{3,1},{4,6},{5,7},{6,4},{7,5},{8,10},{9,11},{10,... | collective-permute-start | bytes 393224 | tf_op jit(solution)/shard_map/ppermute | solution.py:264
  11.4 2.5 %collective-permute-start.2 = (bf16[128,512]{1,0:T(8,128)(2,1)S(1)}, bf16[128,512]{1,0:T(8,128)(2,1)S(1)}, u32[]{:S(2)}, u32[]{:S(2)}) collective-permute-start(bf16[128,512]{1,0:T(8,128)(2,1)S(1)} %collective-permute-done.refs_1_.refs_6_), channel_id=1, source_target_pairs={{0,1},{1,0},{2,3},{3,2},{4,5},{5,4},{6,7},{7,6},{8,9},{9,8},{10,11... | collective-permute-start | bytes 393224 | tf_op jit(solution)/shard_map/ppermute | solution.py:264
  11.4 5.9 %collective-permute-start.1 = (bf16[128,512]{1,0:T(8,128)(2,1)S(1)}, bf16[128,512]{1,0:T(8,128)(2,1)S(1)}, u32[]{:S(2)}, u32[]{:S(2)}) collective-permute-start(bf16[128,512]{1,0:T(8,128)(2,1)S(1)} %collective-permute-done.refs_1_.refs_6_), channel_id=1, source_target_pairs={{0,2},{1,3},{2,0},{3,1},{4,6},{5,7},{6,4},{7,5},{8,10},{9,11},{10,... | collective-permute-start | bytes 393224 | tf_op jit(solution)/shard_map/ppermute | solution.py:264
  13.6 3.7 %collective-permute-start.6 = (bf16[128,512]{1,0:T(8,128)(2,1)S(1)}, bf16[128,512]{1,0:T(8,128)(2,1)S(1)}, u32[]{:S(2)}, u32[]{:S(2)}) collective-permute-start(bf16[128,512]{1,0:T(8,128)(2,1)S(1)} %collective-permute-done.5.refs_1_.refs_8_), channel_id=1, source_target_pairs={{0,1},{1,0},{2,3},{3,2},{4,5},{5,4},{6,7},{7,6},{8,9},{9,8},{10,11... | collective-permute-start | bytes 393224 | tf_op jit(solution)/shard_map/ppermute | solution.py:264
  17.3 1.3 %collective-permute-start.4 = (bf16[128,512]{1,0:T(8,128)(2,1)S(1)}, bf16[128,512]{1,0:T(8,128)(2,1)S(1)}, u32[]{:S(2)}, u32[]{:S(2)}) collective-permute-start(bf16[128,512]{1,0:T(8,128)(2,1)S(1)} %collective-permute-done.1.refs_1_.refs_10_), channel_id=1, source_target_pairs={{0,1},{1,0},{2,3},{3,2},{4,5},{5,4},{6,7},{7,6},{8,9},{9,8},{10,11... | collective-permute-start | bytes 393224 | tf_op jit(solution)/shard_map/ppermute | solution.py:264
  19.7 1.4 %collective-permute-start.7 = (bf16[128,512]{1,0:T(8,128)(2,1)S(1)}, bf16[128,512]{1,0:T(8,128)(2,1)S(1)}, u32[]{:S(2)}, u32[]{:S(2)}) collective-permute-start(bf16[128,512]{1,0:T(8,128)(2,1)S(1)} %get-tuple-element.60), channel_id=1, source_target_pairs={{0,1},{1,0},{2,3},{3,2},{4,5},{5,4},{6,7},{7,6},{8,9},{9,8},{10,11... | collective-permute-start | bytes 393224 | tf_op jit(solution)/shard_map/ppermute | solution.py:264
  20.4 4.6 %collective-permute-start.11 = (bf16[128,512]{1,0:T(8,128)(2,1)S(1)}, bf16[128,512]{1,0:T(8,128)(2,1)S(1)}, u32[]{:S(2)}, u32[]{:S(2)}) collective-permute-start(bf16[128,512]{1,0:T(8,128)(2,1)S(1)} %get-tuple-element.77), channel_id=1, source_target_pairs={{0,1},{1,0},{2,3},{3,2},{4,5},{5,4},{6,7},{7,6},{8,9},{9,8},{10,11... | collective-permute-start | bytes 393224 | tf_op jit(solution)/shard_map/ppermute | solution.py:264
  21.1 5.6 %collective-permute-start.12 = (bf16[128,512]{1,0:T(8,128)(2,1)S(1)}, bf16[128,512]{1,0:T(8,128)(2,1)S(1)}, u32[]{:S(2)}, u32[]{:S(2)}) collective-permute-start(bf16[128,512]{1,0:T(8,128)(2,1)S(1)} %convert_add_fusion.1), channel_id=1, source_target_pairs={{0,2},{1,3},{2,0},{3,1},{4,6},{5,7},{6,4},{7,5},{8,10},{9,11},{10,... | collective-permute-start | bytes 393224 | tf_op jit(solution)/shard_map/ppermute | solution.py:264
  23.1 6.1 %collective-permute-start.8 = (bf16[128,512]{1,0:T(8,128)(2,1)S(1)}, bf16[128,512]{1,0:T(8,128)(2,1)S(1)}, u32[]{:S(2)}, u32[]{:S(2)}) collective-permute-start(bf16[128,512]{1,0:T(8,128)(2,1)S(1)} %get-tuple-element.67), channel_id=1, source_target_pairs={{0,1},{1,0},{2,3},{3,2},{4,5},{5,4},{6,7},{7,6},{8,9},{9,8},{10,11... | collective-permute-start | bytes 393224 | tf_op jit(solution)/shard_map/ppermute | solution.py:264
  23.1 10.1 %collective-permute-start.9 = (bf16[128,512]{1,0:T(8,128)(2,1)S(1)}, bf16[128,512]{1,0:T(8,128)(2,1)S(1)}, u32[]{:S(2)}, u32[]{:S(2)}) collective-permute-start(bf16[128,512]{1,0:T(8,128)(2,1)S(1)} %get-tuple-element.74), channel_id=1, source_target_pairs={{0,1},{1,0},{2,3},{3,2},{4,5},{5,4},{6,7},{7,6},{8,9},{9,8},{10,11... | collective-permute-start | bytes 393224 | tf_op jit(solution)/shard_map/ppermute | solution.py:264
  23.6 7.5 %copy-start = (bf16[1024,512]{1,0:T(8,128)(2,1)S(1)}, bf16[1024,512]{1,0:T(8,128)(2,1)}, u32[]{:S(2)}) copy-start(bf16[1024,512]{1,0:T(8,128)(2,1)} %w_ref.1) | copy-start | bytes 3145732
  26.8 8.6 %collective-permute-start.13 = (bf16[128,512]{1,0:T(8,128)(2,1)S(1)}, bf16[128,512]{1,0:T(8,128)(2,1)S(1)}, u32[]{:S(2)}, u32[]{:S(2)}) collective-permute-start(bf16[128,512]{1,0:T(8,128)(2,1)S(1)} %add_convert_fusion), channel_id=1, source_target_pairs={{0,4},{1,5},{2,6},{3,7},{4,0},{5,1},{6,2},{7,3},{8,12},{9,13},{10,... | collective-permute-start | bytes 393224 | tf_op jit(solution)/shard_map/ppermute | solution.py:264
  29.3 6.5 %collective-permute-start.10 = (bf16[128,512]{1,0:T(8,128)(2,1)S(1)}, bf16[128,512]{1,0:T(8,128)(2,1)S(1)}, u32[]{:S(2)}, u32[]{:S(2)}) collective-permute-start(bf16[128,512]{1,0:T(8,128)(2,1)S(1)} %convert_add_fusion), channel_id=1, source_target_pairs={{0,2},{1,3},{2,0},{3,1},{4,6},{5,7},{6,4},{7,5},{8,10},{9,11},{10,... | collective-permute-start | bytes 393224 | tf_op jit(solution)/shard_map/ppermute | solution.py:264
where the time goes:
time: 36.7 us; the launch traced here: 36.5 us
  starting transfers between devices  13 us (35%)
  Pallas kernels  11.1 us (30%)
  waiting for transfers between devices  10.1 us (28%)
  between operations  1.45 us (4%)
  other arithmetic  0.87 us (2%)
    ppermute x14, starting transfers between devices, trade(): return lax.ppermute(x, 'vid', [(i, i ^ k) for i in range(videos)])  13 us
    ppermute x14, waiting for transfers between devices, trade(): return lax.ppermute(x, 'vid', [(i, i ^ k) for i in range(videos)])  10.1 us
    pallas_call x1, Pallas kernels, embed(): pl.pallas_call(embed_kernel, in_specs=[pl.BlockSpec(memory_space=pl.ANY)]...  3.18 us
    pallas_call x4, Pallas kernels, score(): pl.pallas_call(lambda *refs: score_kernel(k, len(chunk), temper, *refs),...  2.48 us
    pallas_call x1, Pallas kernels, back(): pl.pallas_call(back_kernel, in_specs=[VMEM, VMEM], out_specs=pl.BlockSpec...  2.11 us
    pallas_call x3, Pallas kernels, share(): pl.pallas_call(lambda *refs: share_kernel(ks, *refs), in_specs=[VMEM] * (...  2.05 us
    pallas_call x1, Pallas kernels, rows_of(): pl.pallas_call(lambda *refs: rows_kernel([len(chunk) for chunk in chunks]...  1.3 us
    mul x1, other arithmetic, shards(): return (loss.reshape(-1), frame_grad, sums[0] * temper)  0.77 us
  transfers between devices with their start and end apart: 14, of which 7 were waited for; matrix products, arithmetic and copies ran while one was open for 0% of the time, Pallas kernels for 28%

commit v1 on v0

--- a/solution.py
+++ b/solution.py
@@ -306,6 +306,14 @@
     bit = 1
     while bit < chips:
         for k in range(chips - bit, 0, -2 * bit):
+            if bit == 1 and k > 1:
+                cut = sums[k].shape[0] // 2
+                moved = [
+                    sums[k - 1][at] + trade(sums[k][at].astype(BF16), 2).astype(F32)
+                    for at in (slice(None, cut), slice(cut, None))
+                ]
+                sums[k - 1] = jnp.concatenate(moved, axis=0)
+                continue
             sums[k - bit] = sums[k - bit] + trade(sums[k].astype(BF16), 2 * bit).astype(F32)
         bit *= 2
     frame_grad = back(g, w_frame)

time: 36.7 us -> 37.2 us (1.014)
  starting transfers between devices: 13 us -> 14.2 us
  waiting for transfers between devices: 10.1 us -> 9.23 us
    ppermute x14 -> x15, starting transfers between devices: 13 us -> 14.2 us  [trade(): return lax.ppermute(x, 'vid', [(i, i ^ k) for i in range(videos)])]
    ppermute x14 -> x15, waiting for transfers between devices: 10.1 us -> 9.23 us  [trade(): return lax.ppermute(x, 'vid', [(i, i ^ k) for i in range(videos)])]
  transfers between devices with their start and end apart: 14 -> 15, of which waited for: 7 -> 7; matrix products, arithmetic and copies ran while one was open for 0% -> 0% of each run, Pallas kernels for 28% -> 27%
where the time goes in v1:
time: 37.2 us; the launch traced here: 37 us
  starting transfers between devices  14.2 us (38%)
  Pallas kernels  11.1 us (30%)
  waiting for transfers between devices  9.23 us (25%)
  between operations  1.48 us (4%)
  other arithmetic  0.9 us (2%)
    ppermute x15, starting transfers between devices, trade(): return lax.ppermute(x, 'vid', [(i, i ^ k) for i in range(videos)])  14.2 us
    ppermute x15, waiting for transfers between devices, trade(): return lax.ppermute(x, 'vid', [(i, i ^ k) for i in range(videos)])  9.23 us
    pallas_call x1, Pallas kernels, embed(): pl.pallas_call(embed_kernel, in_specs=[pl.BlockSpec(memory_space=pl.ANY)]...  3.18 us
    pallas_call x4, Pallas kernels, score(): pl.pallas_call(lambda *refs: score_kernel(k, len(chunk), temper, *refs),...  2.48 us
    pallas_call x1, Pallas kernels, back(): pl.pallas_call(back_kernel, in_specs=[VMEM, VMEM], out_specs=pl.BlockSpec...  2.12 us
    pallas_call x3, Pallas kernels, share(): pl.pallas_call(lambda *refs: share_kernel(ks, *refs), in_specs=[VMEM] * (...  2.05 us
    pallas_call x1, Pallas kernels, rows_of(): pl.pallas_call(lambda *refs: rows_kernel([len(chunk) for chunk in chunks]...  1.31 us
    mul x1, other arithmetic, shards(): return (loss.reshape(-1), frame_grad, sums[0] * temper)  0.77 us
  transfers between devices with their start and end apart: 15, of which 7 were waited for; matrix products, arithmetic and copies ran while one was open for 0% of the time, Pallas kernels for 27%

profile of v1, /device:TPU:0, one launch (start us, length us, event | category | flops | bytes accessed | tf_op | source)
XLA Modules:
  0.0 37.0 jit_solution(7306437153755201542)
XLA Ops:
  0.7 4.1 %collective-permute-start = (bf16[128,512]{1,0:T(8,128)(2,1)}, bf16[128,512]{1,0:T(8,128)(2,1)S(1)}, u32[]{:S(2)}, u32[]{:S(2)}) collective-permute-start(bf16[128,512]{1,0:T(8,128)(2,1)} %refs_4_.2), channel_id=1, source_target_pairs={{0,4},{1,5},{2,6},{3,7},{4,0},{5,1},{6,2},{7,3},{8,12},{9,13},{10,... | collective-permute-start | bytes 393224 | tf_op jit(solution)/shard_map/ppermute | solution.py:264
  4.8 0.0 collective-permute-start.3
  4.8 1.6 %collective-permute-start.5 = (bf16[128,512]{1,0:T(8,128)(2,1)}, bf16[128,512]{1,0:T(8,128)(2,1)S(1)}, u32[]{:S(2)}, u32[]{:S(2)}) collective-permute-start(bf16[128,512]{1,0:T(8,128)(2,1)} %refs_4_.2), channel_id=1, source_target_pairs={{0,2},{1,3},{2,0},{3,1},{4,6},{5,7},{6,4},{7,5},{8,10},{9,11},{10,... | collective-permute-start | bytes 393224 | tf_op jit(solution)/shard_map/ppermute | solution.py:264
  6.4 3.2 %embed.1.refs_0_.refs_2_ = bf16[1024,512]{1,0:T(8,128)(2,1)S(1)} custom-call(bf16[1024,1024]{1,0:T(8,128)(2,1)} %x_hbm.1, bf16[1024,512]{1,0:T(8,128)(2,1)} %w_ref.1), custom_call_target="tpu_custom_call" | custom-call | flops 1073741824 | bytes 4194304 | tf_op jit(solution)/shard_map/embed/pallas_call | solution.py:54
  9.5 1.9 %collective-permute-done.refs_1_.refs_6_ = bf16[128,512]{1,0:T(8,128)(2,1)S(1)} collective-permute-done((bf16[128,512]{1,0:T(8,128)(2,1)}, bf16[128,512]{1,0:T(8,128)(2,1)S(1)}, u32[]{:S(2)}, u32[]{:S(2)}) %collective-permute-start) | collective-permute-done | bytes 131104 | tf_op jit(solution)/shard_map/ppermute | solution.py:264
  11.4 0.0 collective-permute-start.2
  11.4 0.8 %collective-permute-start.1 = (bf16[128,512]{1,0:T(8,128)(2,1)S(1)}, bf16[128,512]{1,0:T(8,128)(2,1)S(1)}, u32[]{:S(2)}, u32[]{:S(2)}) collective-permute-start(bf16[128,512]{1,0:T(8,128)(2,1)S(1)} %collective-permute-done.refs_1_.refs_6_), channel_id=1, source_target_pairs={{0,2},{1,3},{2,0},{3,1},{4,6},{5,7},{6,4},{7,5},{8,10},{9,11},{10,... | collective-permute-start | bytes 393224 | tf_op jit(solution)/shard_map/ppermute | solution.py:264
  12.9 0.7 %score_0.1 = (f32[256,1024]{1,0:T(8,128)S(1)}, f32[1,1024]{1,0:T(1,128)S(1)}, f32[1,1024]{1,0:T(1,128)S(1)}, f32[1,1024]{1,0:T(1,128)S(1)}, f32[8,1024]{1,0:T(8,128)S(1)}) custom-call(bf16[1024,512]{1,0:T(8,128)(2,1)S(1)} %embed.1.refs_0_.refs_2_, bf16[128,512]{1,0:T(8,128)(2,1)S(1)} %copy-done.1, ...), custom_call_target="tpu_custom_call" | custom-call | flops 268435456 | bytes 2359296 | tf_op jit(solution)/shard_map/score_0/pallas_call | solution.py:132
  13.6 0.3 collective-permute-start.6
  13.9 0.6 %score_2.1 = (f32[256,1024]{1,0:T(8,128)S(1)}, f32[1,1024]{1,0:T(1,128)S(1)}, f32[1,1024]{1,0:T(1,128)S(1)}) custom-call(bf16[1024,512]{1,0:T(8,128)(2,1)S(1)} %embed.1.refs_0_.refs_2_, bf16[128,512]{1,0:T(8,128)(2,1)S(1)} %collective-permute-done.refs_1_.refs_6_, bf16[128,512]{1,0:T(8,128)(2,1)S(1)} %collective-permute-done.2.refs_2_.refs_7_, ...), custom_call_target="tpu_custom_call" | custom-call | flops 268435456 | bytes 2359296 | tf_op jit(solution)/shard_map/score_2/pallas_call | solution.py:132
  14.5 2.8 %collective-permute-done.1.refs_1_.refs_10_ = bf16[128,512]{1,0:T(8,128)(2,1)S(1)} collective-permute-done((bf16[128,512]{1,0:T(8,128)(2,1)S(1)}, bf16[128,512]{1,0:T(8,128)(2,1)S(1)}, u32[]{:S(2)}, u32[]{:S(2)}) %collective-permute-start.1) | collective-permute-done | bytes 131104 | tf_op jit(solution)/shard_map/ppermute | solution.py:264
  17.3 0.6 %score_1.1 = (f32[256,1024]{1,0:T(8,128)S(1)}, f32[1,1024]{1,0:T(1,128)S(1)}, f32[1,1024]{1,0:T(1,128)S(1)}) custom-call(bf16[1024,512]{1,0:T(8,128)(2,1)S(1)} %embed.1.refs_0_.refs_2_, bf16[128,512]{1,0:T(8,128)(2,1)S(1)} %collective-permute-done.5.refs_1_.refs_8_, bf16[128,512]{1,0:T(8,128)(2,1)S(1)} %collective-permute-done.6.refs_2_.refs_9_, ...), custom_call_target="tpu_custom_call" | custom-call | flops 268435456 | bytes 2359296 | tf_op jit(solution)/shard_map/score_1/pallas_call | solution.py:132
  17.9 0.8 %collective-permute-done.4.refs_2_.refs_11_ = bf16[128,512]{1,0:T(8,128)(2,1)S(1)} collective-permute-done((bf16[128,512]{1,0:T(8,128)(2,1)S(1)}, bf16[128,512]{1,0:T(8,128)(2,1)S(1)}, u32[]{:S(2)}, u32[]{:S(2)}) %collective-permute-start.4) | collective-permute-done | bytes 131104 | tf_op jit(solution)/shard_map/ppermute | solution.py:264
  18.7 0.6 %score_3.1 = (f32[256,1024]{1,0:T(8,128)S(1)}, f32[1,1024]{1,0:T(1,128)S(1)}, f32[1,1024]{1,0:T(1,128)S(1)}) custom-call(bf16[1024,512]{1,0:T(8,128)(2,1)S(1)} %embed.1.refs_0_.refs_2_, bf16[128,512]{1,0:T(8,128)(2,1)S(1)} %collective-permute-done.1.refs_1_.refs_10_, bf16[128,512]{1,0:T(8,128)(2,1)S(1)} %collective-permute-done.4.refs_2_.refs_11_, ...), custom_call_target="tpu_custom_call" | custom-call | flops 268435456 | bytes 2359296 | tf_op jit(solution)/shard_map/score_3/pallas_call | solution.py:132
  19.2 0.4 %share_3.1 = (bf16[256,1024]{1,0:T(8,128)(2,1)S(1)}, f32[128,512]{1,0:T(8,128)S(1)}, bf16[128,512]{1,0:T(8,128)(2,1)S(1)}) custom-call(f32[1,1024]{1,0:T(1,128)S(1)} %get-tuple-element.51.refs_0_.refs_4_, f32[1,1024]{1,0:T(1,128)S(1)} %get-tuple-element.52.refs_1_, bf16[1024,512]{1,0:T(8,128)(2,1)S(1)} %embed.1.refs_0_.refs_2_, ...), custom_call_target="tpu_custom_call" | custom-call | flops 268435456 | bytes 2621440 | tf_op jit(solution)/shard_map/share_3/pallas_call | solution.py:182
  19.7 0.2 collective-permute-start.7
  19.9 0.5 %share_2.1 = (bf16[256,1024]{1,0:T(8,128)(2,1)S(1)}, f32[128,512]{1,0:T(8,128)S(1)}, bf16[128,512]{1,0:T(8,128)(2,1)S(1)}) custom-call(f32[1,1024]{1,0:T(1,128)S(1)} %get-tuple-element.51.refs_0_.refs_4_, f32[1,1024]{1,0:T(1,128)S(1)} %get-tuple-element.52.refs_1_, bf16[1024,512]{1,0:T(8,128)(2,1)S(1)} %embed.1.refs_0_.refs_2_, ...), custom_call_target="tpu_custom_call" | custom-call | flops 268435456 | bytes 2621440 | tf_op jit(solution)/shard_map/share_2/pallas_call | solution.py:182
  20.4 0.4 %collective-permute-start.11 = (bf16[128,512]{1,0:T(8,128)(2,1)S(1)}, bf16[128,512]{1,0:T(8,128)(2,1)S(1)}, u32[]{:S(2)}, u32[]{:S(2)}) collective-permute-start(bf16[128,512]{1,0:T(8,128)(2,1)S(1)} %get-tuple-element.77), channel_id=1, source_target_pairs={{0,1},{1,0},{2,3},{3,2},{4,5},{5,4},{6,7},{7,6},{8,9},{9,8},{10,11... | collective-permute-start | bytes 393224 | tf_op jit(solution)/shard_map/ppermute | solution.py:264
  20.8 0.3 collective-permute-done.7
  21.2 0.8 %collective-permute-start.12 = (bf16[64,512]{1,0:T(8,128)(2,1)S(1)}, bf16[64,512]{1,0:T(8,128)(2,1)S(1)}, u32[]{:S(2)}, u32[]{:S(2)}) collective-permute-start(bf16[64,512]{1,0:T(8,128)(2,1)S(1)} %get-tuple-element.81), channel_id=1, source_target_pairs={{0,2},{1,3},{2,0},{3,1},{4,6},{5,7},{6,4},{7,5},{8,10},{9,11},{10,... | collective-permute-start | bytes 196616 | tf_op jit(solution)/shard_map/ppermute | solution.py:264
  22.0 1.3 %collective-permute-start.13 = (bf16[64,512]{1,0:T(8,128)(2,1)S(1)}, bf16[64,512]{1,0:T(8,128)(2,1)S(1)}, u32[]{:S(2)}, u32[]{:S(2)}) collective-permute-start(bf16[64,512]{1,0:T(8,128)(2,1)S(1)} %get-tuple-element.82), channel_id=1, source_target_pairs={{0,2},{1,3},{2,0},{3,1},{4,6},{5,7},{6,4},{7,5},{8,10},{9,11},{10,... | collective-permute-start | bytes 196616 | tf_op jit(solution)/shard_map/ppermute | solution.py:264
  23.3 1.1 %share_1.1 = (bf16[256,1024]{1,0:T(8,128)(2,1)S(1)}, f32[128,512]{1,0:T(8,128)S(1)}, bf16[128,512]{1,0:T(8,128)(2,1)S(1)}, bf16[256,1024]{1,0:T(8,128)(2,1)S(1)}...) custom-call(f32[1,1024]{1,0:T(1,128)S(1)} %get-tuple-element.51.refs_0_.refs_4_, ...), custom_call_target="tpu_custom_call" | custom-call | flops 536870912 | bytes 4194304 | tf_op jit(solution)/shard_map/share_1/pallas_call | solution.py:182
  24.4 0.5 %collective-permute-start.9 = (bf16[128,512]{1,0:T(8,128)(2,1)S(1)}, bf16[128,512]{1,0:T(8,128)(2,1)S(1)}, u32[]{:S(2)}, u32[]{:S(2)}) collective-permute-start(bf16[128,512]{1,0:T(8,128)(2,1)S(1)} %get-tuple-element.74), channel_id=1, source_target_pairs={{0,1},{1,0},{2,3},{3,2},{4,5},{5,4},{6,7},{7,6},{8,9},{9,8},{10,11... | collective-permute-start | bytes 393224 | tf_op jit(solution)/shard_map/ppermute | solution.py:264
  24.9 0.0 copy-start
  25.0 1.3 %rows.1.g_ref = bf16[1024,512]{1,0:T(8,128)(2,1)S(1)} custom-call(bf16[256,1024]{1,0:T(8,128)(2,1)S(1)} %get-tuple-element.68.refs_0_, bf16[256,1024]{1,0:T(8,128)(2,1)S(1)} %get-tuple-element.69.refs_1_, bf16[256,1024]{1,0:T(8,128)(2,1)S(1)} %get-tuple-element.70.refs_2_, bf16[256,1024]{1,0:T(8,128)(2,1)S(1)} %get-tuple-element.71.refs_3_, ...), custom_call_target="tpu_custom_call" | custom-call | flops 1073741824 | bytes 3145728 | tf_op jit(solution)/shard_map/rows/pallas_call | solution.py:216
  26.3 0.5 %collective-permute-done.13 = bf16[64,512]{1,0:T(8,128)(2,1)S(1)} collective-permute-done((bf16[64,512]{1,0:T(8,128)(2,1)S(1)}, bf16[64,512]{1,0:T(8,128)(2,1)S(1)}, u32[]{:S(2)}, u32[]{:S(2)}) %collective-permute-start.13) | collective-permute-done | bytes 65568 | tf_op jit(solution)/shard_map/ppermute | solution.py:264
  26.8 2.9 %collective-permute-start.14 = (bf16[128,512]{1,0:T(8,128)(2,1)S(1)}, bf16[128,512]{1,0:T(8,128)(2,1)S(1)}, u32[]{:S(2)}, u32[]{:S(2)}) collective-permute-start(bf16[128,512]{1,0:T(8,128)(2,1)S(1)} %pad_maximum_fusion), channel_id=1, source_target_pairs={{0,4},{1,5},{2,6},{3,7},{4,0},{5,1},{6,2},{7,3},{8,12},{9,13},{10,... | collective-permute-start | bytes 393224 | tf_op jit(solution)/shard_map/ppermute | solution.py:264
  29.8 1.3 %collective-permute-start.10 = (bf16[128,512]{1,0:T(8,128)(2,1)S(1)}, bf16[128,512]{1,0:T(8,128)(2,1)S(1)}, u32[]{:S(2)}, u32[]{:S(2)}) collective-permute-start(bf16[128,512]{1,0:T(8,128)(2,1)S(1)} %convert_add_fusion.1), channel_id=1, source_target_pairs={{0,2},{1,3},{2,0},{3,1},{4,6},{5,7},{6,4},{7,5},{8,10},{9,11},{10,... | collective-permute-start | bytes 393224 | tf_op jit(solution)/shard_map/ppermute | solution.py:264
  31.1 2.1 %back.1 = bf16[1024,1024]{1,0:T(8,128)(2,1)} custom-call(bf16[1024,512]{1,0:T(8,128)(2,1)S(1)} %rows.1.g_ref, bf16[1024,512]{1,0:T(8,128)(2,1)S(1)} %copy-done), custom_call_target="tpu_custom_call" | custom-call | flops 1073741824 | bytes 4194304 | tf_op jit(solution)/shard_map/back/pallas_call | solution.py:245
  33.2 2.4 %collective-permute-done.14 = bf16[128,512]{1,0:T(8,128)(2,1)S(1)} collective-permute-done((bf16[128,512]{1,0:T(8,128)(2,1)S(1)}, bf16[128,512]{1,0:T(8,128)(2,1)S(1)}, u32[]{:S(2)}, u32[]{:S(2)}) %collective-permute-start.14) | collective-permute-done | bytes 131104 | tf_op jit(solution)/shard_map/ppermute | solution.py:264
  35.6 0.6 %collective-permute-done.10 = bf16[128,512]{1,0:T(8,128)(2,1)S(1)} collective-permute-done((bf16[128,512]{1,0:T(8,128)(2,1)S(1)}, bf16[128,512]{1,0:T(8,128)(2,1)S(1)}, u32[]{:S(2)}, u32[]{:S(2)}) %collective-permute-start.10) | collective-permute-done | bytes 131104 | tf_op jit(solution)/shard_map/ppermute | solution.py:264
  36.2 0.8 %add_multiply_fusion = f32[128,512]{1,0:T(8,128)} fusion(bf16[128,512]{1,0:T(8,128)(2,1)S(1)} %collective-permute-done.14, bf16[128,512]{1,0:T(8,128)(2,1)S(1)} %collective-permute-done.10, f32[128,512]{1,0:T(8,128)S(1)} %get-tuple-element.73, bf16[128,512]{1,0:T(8,128)(2,1)S(1)} %collective-permute-done.9), kind=kLoop, calls=%fused_computation | loop fusion | flops 458752 | bytes 917504 | tf_op jit(solution)/shard_map/mul | solution.py:320
  (25 shorter events, 0.2 us)
Async XLA Ops:
  0.6 12.2 %copy-start.1 = (bf16[128,512]{1,0:T(8,128)(2,1)S(1)}, bf16[128,512]{1,0:T(8,128)(2,1)}, u32[]{:S(2)}) copy-start(bf16[128,512]{1,0:T(8,128)(2,1)} %refs_4_.2) | copy-start | bytes 393220
  0.6 12.2 %copy-start.2 = (s32[1024]{0:T(1024)S(1)}, s32[1024]{0:T(1024)}, u32[]{:S(2)}) copy-start(s32[1024]{0:T(1024)} %param.10) | copy-start | bytes 12292
  0.7 12.2 %copy-start.3 = (s32[1,64]{1,0:T(1,128)S(1)}, s32[1,64]{1,0:T(1,128)}, u32[]{:S(2)}) copy-start(s32[1,64]{1,0:T(1,128)} %refs_5_.1) | copy-start | bytes 772
  0.7 12.2 %copy-start.4 = (s32[1,64]{1,0:T(1,128)S(1)}, s32[1,64]{1,0:T(1,128)}, u32[]{:S(2)}) copy-start(s32[1,64]{1,0:T(1,128)} %refs_6_.1) | copy-start | bytes 772
  0.7 10.7 %collective-permute-start = (bf16[128,512]{1,0:T(8,128)(2,1)}, bf16[128,512]{1,0:T(8,128)(2,1)S(1)}, u32[]{:S(2)}, u32[]{:S(2)}) collective-permute-start(bf16[128,512]{1,0:T(8,128)(2,1)} %refs_4_.2), channel_id=1, source_target_pairs={{0,4},{1,5},{2,6},{3,7},{4,0},{5,1},{6,2},{7,3},{8,12},{9,13},{10,... | collective-permute-start | bytes 393224 | tf_op jit(solution)/shard_map/ppermute | solution.py:264
  4.8 8.1 %collective-permute-start.3 = (bf16[128,512]{1,0:T(8,128)(2,1)}, bf16[128,512]{1,0:T(8,128)(2,1)S(1)}, u32[]{:S(2)}, u32[]{:S(2)}) collective-permute-start(bf16[128,512]{1,0:T(8,128)(2,1)} %refs_4_.2), channel_id=1, source_target_pairs={{0,1},{1,0},{2,3},{3,2},{4,5},{5,4},{6,7},{7,6},{8,9},{9,8},{10,11... | collective-permute-start | bytes 393224 | tf_op jit(solution)/shard_map/ppermute | solution.py:264
  4.8 8.8 %collective-permute-start.5 = (bf16[128,512]{1,0:T(8,128)(2,1)}, bf16[128,512]{1,0:T(8,128)(2,1)S(1)}, u32[]{:S(2)}, u32[]{:S(2)}) collective-permute-start(bf16[128,512]{1,0:T(8,128)(2,1)} %refs_4_.2), channel_id=1, source_target_pairs={{0,2},{1,3},{2,0},{3,1},{4,6},{5,7},{6,4},{7,5},{8,10},{9,11},{10,... | collective-permute-start | bytes 393224 | tf_op jit(solution)/shard_map/ppermute | solution.py:264
  11.4 2.5 %collective-permute-start.2 = (bf16[128,512]{1,0:T(8,128)(2,1)S(1)}, bf16[128,512]{1,0:T(8,128)(2,1)S(1)}, u32[]{:S(2)}, u32[]{:S(2)}) collective-permute-start(bf16[128,512]{1,0:T(8,128)(2,1)S(1)} %collective-permute-done.refs_1_.refs_6_), channel_id=1, source_target_pairs={{0,1},{1,0},{2,3},{3,2},{4,5},{5,4},{6,7},{7,6},{8,9},{9,8},{10,11... | collective-permute-start | bytes 393224 | tf_op jit(solution)/shard_map/ppermute | solution.py:264
  11.4 5.9 %collective-permute-start.1 = (bf16[128,512]{1,0:T(8,128)(2,1)S(1)}, bf16[128,512]{1,0:T(8,128)(2,1)S(1)}, u32[]{:S(2)}, u32[]{:S(2)}) collective-permute-start(bf16[128,512]{1,0:T(8,128)(2,1)S(1)} %collective-permute-done.refs_1_.refs_6_), channel_id=1, source_target_pairs={{0,2},{1,3},{2,0},{3,1},{4,6},{5,7},{6,4},{7,5},{8,10},{9,11},{10,... | collective-permute-start | bytes 393224 | tf_op jit(solution)/shard_map/ppermute | solution.py:264
  13.6 3.7 %collective-permute-start.6 = (bf16[128,512]{1,0:T(8,128)(2,1)S(1)}, bf16[128,512]{1,0:T(8,128)(2,1)S(1)}, u32[]{:S(2)}, u32[]{:S(2)}) collective-permute-start(bf16[128,512]{1,0:T(8,128)(2,1)S(1)} %collective-permute-done.5.refs_1_.refs_8_), channel_id=1, source_target_pairs={{0,1},{1,0},{2,3},{3,2},{4,5},{5,4},{6,7},{7,6},{8,9},{9,8},{10,11... | collective-permute-start | bytes 393224 | tf_op jit(solution)/shard_map/ppermute | solution.py:264
  17.3 1.3 %collective-permute-start.4 = (bf16[128,512]{1,0:T(8,128)(2,1)S(1)}, bf16[128,512]{1,0:T(8,128)(2,1)S(1)}, u32[]{:S(2)}, u32[]{:S(2)}) collective-permute-start(bf16[128,512]{1,0:T(8,128)(2,1)S(1)} %collective-permute-done.1.refs_1_.refs_10_), channel_id=1, source_target_pairs={{0,1},{1,0},{2,3},{3,2},{4,5},{5,4},{6,7},{7,6},{8,9},{9,8},{10,11... | collective-permute-start | bytes 393224 | tf_op jit(solution)/shard_map/ppermute | solution.py:264
  19.7 1.4 %collective-permute-start.7 = (bf16[128,512]{1,0:T(8,128)(2,1)S(1)}, bf16[128,512]{1,0:T(8,128)(2,1)S(1)}, u32[]{:S(2)}, u32[]{:S(2)}) collective-permute-start(bf16[128,512]{1,0:T(8,128)(2,1)S(1)} %get-tuple-element.60), channel_id=1, source_target_pairs={{0,1},{1,0},{2,3},{3,2},{4,5},{5,4},{6,7},{7,6},{8,9},{9,8},{10,11... | collective-permute-start | bytes 393224 | tf_op jit(solution)/shard_map/ppermute | solution.py:264
  20.4 4.5 %collective-permute-start.11 = (bf16[128,512]{1,0:T(8,128)(2,1)S(1)}, bf16[128,512]{1,0:T(8,128)(2,1)S(1)}, u32[]{:S(2)}, u32[]{:S(2)}) collective-permute-start(bf16[128,512]{1,0:T(8,128)(2,1)S(1)} %get-tuple-element.77), channel_id=1, source_target_pairs={{0,1},{1,0},{2,3},{3,2},{4,5},{5,4},{6,7},{7,6},{8,9},{9,8},{10,11... | collective-permute-start | bytes 393224 | tf_op jit(solution)/shard_map/ppermute | solution.py:264
  21.2 5.1 %collective-permute-start.12 = (bf16[64,512]{1,0:T(8,128)(2,1)S(1)}, bf16[64,512]{1,0:T(8,128)(2,1)S(1)}, u32[]{:S(2)}, u32[]{:S(2)}) collective-permute-start(bf16[64,512]{1,0:T(8,128)(2,1)S(1)} %get-tuple-element.81), channel_id=1, source_target_pairs={{0,2},{1,3},{2,0},{3,1},{4,6},{5,7},{6,4},{7,5},{8,10},{9,11},{10,... | collective-permute-start | bytes 196616 | tf_op jit(solution)/shard_map/ppermute | solution.py:264
  22.0 4.8 %collective-permute-start.13 = (bf16[64,512]{1,0:T(8,128)(2,1)S(1)}, bf16[64,512]{1,0:T(8,128)(2,1)S(1)}, u32[]{:S(2)}, u32[]{:S(2)}) collective-permute-start(bf16[64,512]{1,0:T(8,128)(2,1)S(1)} %get-tuple-element.82), channel_id=1, source_target_pairs={{0,2},{1,3},{2,0},{3,1},{4,6},{5,7},{6,4},{7,5},{8,10},{9,11},{10,... | collective-permute-start | bytes 196616 | tf_op jit(solution)/shard_map/ppermute | solution.py:264
  24.4 5.3 %collective-permute-start.8 = (bf16[128,512]{1,0:T(8,128)(2,1)S(1)}, bf16[128,512]{1,0:T(8,128)(2,1)S(1)}, u32[]{:S(2)}, u32[]{:S(2)}) collective-permute-start(bf16[128,512]{1,0:T(8,128)(2,1)S(1)} %get-tuple-element.67), channel_id=1, source_target_pairs={{0,1},{1,0},{2,3},{3,2},{4,5},{5,4},{6,7},{7,6},{8,9},{9,8},{10,11... | collective-permute-start | bytes 393224 | tf_op jit(solution)/shard_map/ppermute | solution.py:264
  24.4 8.8 %collective-permute-start.9 = (bf16[128,512]{1,0:T(8,128)(2,1)S(1)}, bf16[128,512]{1,0:T(8,128)(2,1)S(1)}, u32[]{:S(2)}, u32[]{:S(2)}) collective-permute-start(bf16[128,512]{1,0:T(8,128)(2,1)S(1)} %get-tuple-element.74), channel_id=1, source_target_pairs={{0,1},{1,0},{2,3},{3,2},{4,5},{5,4},{6,7},{7,6},{8,9},{9,8},{10,11... | collective-permute-start | bytes 393224 | tf_op jit(solution)/shard_map/ppermute | solution.py:264
  24.9 6.2 %copy-start = (bf16[1024,512]{1,0:T(8,128)(2,1)S(1)}, bf16[1024,512]{1,0:T(8,128)(2,1)}, u32[]{:S(2)}) copy-start(bf16[1024,512]{1,0:T(8,128)(2,1)} %w_ref.1) | copy-start | bytes 3145732
  26.8 8.8 %collective-permute-start.14 = (bf16[128,512]{1,0:T(8,128)(2,1)S(1)}, bf16[128,512]{1,0:T(8,128)(2,1)S(1)}, u32[]{:S(2)}, u32[]{:S(2)}) collective-permute-start(bf16[128,512]{1,0:T(8,128)(2,1)S(1)} %pad_maximum_fusion), channel_id=1, source_target_pairs={{0,4},{1,5},{2,6},{3,7},{4,0},{5,1},{6,2},{7,3},{8,12},{9,13},{10,... | collective-permute-start | bytes 393224 | tf_op jit(solution)/shard_map/ppermute | solution.py:264
  29.8 6.5 %collective-permute-start.10 = (bf16[128,512]{1,0:T(8,128)(2,1)S(1)}, bf16[128,512]{1,0:T(8,128)(2,1)S(1)}, u32[]{:S(2)}, u32[]{:S(2)}) collective-permute-start(bf16[128,512]{1,0:T(8,128)(2,1)S(1)} %convert_add_fusion.1), channel_id=1, source_target_pairs={{0,2},{1,3},{2,0},{3,1},{4,6},{5,7},{6,4},{7,5},{8,10},{9,11},{10,... | collective-permute-start | bytes 393224 | tf_op jit(solution)/shard_map/ppermute | solution.py:264
